TPU v7x, 128 devices: a whole 4x4x4 slice. The times are simulated.
128 devices in a mesh: seq: 64 (over x, y, z_lo, core), fsdp: 2 (over z_hi).
Axes of the slice: x: 4, y: 4, z: 4 (z_hi: 2, z_lo: 2; z = z_hi * 2 + z_lo), core: 2. Of those that a mesh axis runs over, the one named last changes fastest.
Arguments:
- queries: bfloat16 [2, 8192, 8192], P('fsdp', 'seq'), may hold values from -10 to 10
- keys: bfloat16 [2, 8192, 1024], P('fsdp', 'seq'), may hold values from -10 to 10
- values: bfloat16 [2, 8192, 1024], P('fsdp', 'seq'), may hold values from -6 to 6
- out_grad: bfloat16 [2, 8192, 8192], P('fsdp', 'seq'), may hold values from -6 to 6
- doc_lengths: int32 [2, 64], P('fsdp'), may hold values from 1 to 1024, 8192 in all within a row
- inputs: bfloat16 [2, 8192, 4096], P('fsdp', 'seq'), may hold values from -16 to 16
- value_weight: bfloat16 [4096, 1024], P('fsdp'), may hold values from -0.1875 to 0.1875
Outputs:
- grad_queries: bfloat16 [2, 8192, 8192], P('fsdp', 'seq')
- grad_keys: bfloat16 [2, 8192, 1024], P('fsdp', 'seq')
- grad_values: bfloat16 [2, 8192, 1024], P('fsdp', 'seq')
- grad_inputs: bfloat16 [2, 8192, 4096], P('fsdp', 'seq')
- grad_weight: float32 [4096, 1024], P(('seq', 'fsdp'))
Inputs may be any that keep to these rules, and one draw needn't show every extreme that they name: `doc_lengths`: each row lists the lengths of the 64 documents packed into one sequence, in order; they sum to 8192 and the longest is exactly 1024.
All inputs are finite; a program needn't handle non-finite values.
Results may differ from a plain program's by a relative error of at most 0.0079.
Values may be sent and summed in bfloat16 or wider, within the bound.
A program may use at most 192 MiB of HBM per device.

v0:
```python
import math

import jax
import jax.numpy as jnp
from jax import lax
from jax.sharding import PartitionSpec as P

HEADS = 64
KV_HEADS = 8
HEAD_DIM = 128
MAXDOC = 1024


masked_value = -1e30


def shifted(value, axis, by):
    length = lax.axis_size(axis)
    pairs = [(i, i + by) for i in range(length) if 0 <= i + by < length]
    return lax.ppermute(value, axis, pairs)


def in_order(pieces, dim):
    shape = list(pieces.shape[1:])
    shape[dim] *= pieces.shape[0]
    return jnp.moveaxis(pieces, 0, dim).reshape(shape)


def piecewise(value, axis, dim, apply, out_dim):
    size, rows = (lax.axis_size(axis), value.shape[dim])
    count = 2 if rows % 2 == 0 else 1
    done, length = ([], rows // count)
    for k in range(count):
        piece = lax.slice_in_dim(value, k * length, (k + 1) * length, axis=dim)
        starts = jnp.arange(size) * rows + k * length
        done.append(jax.vmap(apply)(lax.all_gather(piece, axis), starts))
    return in_order(jnp.concatenate(done, axis=out_dim + 1), out_dim)


def document_ids(lengths, seqlen_value):
    bounds = jnp.cumsum(lengths)
    positions = jnp.arange(seqlen_value, dtype=jnp.int32)
    return jnp.sum((positions[:, None] >= bounds[None, :]).astype(jnp.int32), axis=1)


def group_backward(query_group, grad_group, key_slab, value_slab, allowed, score_scale):
    scores = (
        jnp.einsum("qhd,kd->hqk", query_group, key_slab, preferred_element_type=jnp.float32)
        * score_scale
    )
    scores = jnp.where(allowed[None], scores, masked_value)
    row_max = jnp.max(scores, axis=2, keepdims=True)
    weights = jnp.where(allowed[None], jnp.exp(scores - row_max), 0.0)
    probs = weights / jnp.sum(weights, axis=2, keepdims=True)
    dprob = jnp.einsum("qhd,kd->hqk", grad_group, value_slab, preferred_element_type=jnp.float32)
    row_delta = jnp.sum(probs * dprob, axis=2, keepdims=True)
    dscore = (probs * (dprob - row_delta)).astype(jnp.bfloat16)
    probs_low = probs.astype(jnp.bfloat16)
    query_grad = (
        jnp.einsum("hqk,kd->qhd", dscore, key_slab, preferred_element_type=jnp.float32)
        * score_scale
    ).astype(jnp.bfloat16)
    key_part = (
        jnp.einsum("hqk,qhd->kd", dscore, query_group, preferred_element_type=jnp.float32)
        * score_scale
    )
    value_part = jnp.einsum(
        "hqk,qhd->kd", probs_low, grad_group, preferred_element_type=jnp.float32
    )
    return (query_grad, key_part, value_part)


def local(queries, keys, values, out_grad, doc_lengths, inputs, value_weight):
    seq_count = lax.axis_size("seq")
    fsdp_count = lax.axis_size("fsdp")
    tok_rows = queries.shape[1]
    head_width = HEAD_DIM
    seq_total = tok_rows * seq_count
    group_size = HEADS // KV_HEADS
    query_local = queries[0]
    grad_local = out_grad[0]
    doc_ids = document_ids(doc_lengths[0], seq_total)
    reach_blocks = MAXDOC // tok_rows
    slab_rows = (reach_blocks + 1) * tok_rows
    device_index = lax.axis_index("seq")
    current = jnp.stack((keys[0], values[0]))
    received = [current]
    for hop_count in range(reach_blocks):
        current = shifted(current, "seq", 1)
        received.append(current)
    slab_pair = jnp.concatenate(received[::-1], axis=1)
    pad_docs = jnp.concatenate(
        [jnp.full((reach_blocks * tok_rows,), -1, jnp.int32), doc_ids], axis=0
    )
    key_docs = lax.dynamic_slice_in_dim(pad_docs, device_index * tok_rows, slab_rows, 0)
    query_docs = lax.dynamic_slice_in_dim(doc_ids, device_index * tok_rows, tok_rows, 0)
    query_offsets = jnp.arange(tok_rows, dtype=jnp.int32)
    key_offsets = jnp.arange(slab_rows, dtype=jnp.int32)
    allowed = (query_docs[:, None] == key_docs[None, :]) & (
        key_offsets[None, :] <= query_offsets[:, None] + reach_blocks * tok_rows
    )
    score_scale = 1.0 / math.sqrt(head_width)
    query_groups = jnp.transpose(
        query_local.reshape(tok_rows, KV_HEADS, group_size, head_width), (1, 0, 2, 3)
    )
    grad_groups = jnp.transpose(
        grad_local.reshape(tok_rows, KV_HEADS, group_size, head_width), (1, 0, 2, 3)
    )
    key_slabs = jnp.transpose(slab_pair[0].reshape(slab_rows, KV_HEADS, head_width), (1, 0, 2))
    value_slabs = jnp.transpose(slab_pair[1].reshape(slab_rows, KV_HEADS, head_width), (1, 0, 2))

    def one_group(operands):
        return group_backward(
            operands[0], operands[1], operands[2], operands[3], allowed, score_scale
        )

    query_grads, key_parts, value_parts = lax.map(
        one_group, (query_groups, grad_groups, key_slabs, value_slabs)
    )
    query_back = jnp.transpose(query_grads, (1, 0, 2, 3)).reshape(tok_rows, HEADS * head_width)
    key_rows = jnp.transpose(key_parts, (1, 0, 2)).reshape(slab_rows, KV_HEADS * head_width)
    value_rows = jnp.transpose(value_parts, (1, 0, 2)).reshape(slab_rows, KV_HEADS * head_width)
    part_pair = jnp.stack((key_rows, value_rows))
    carried = part_pair[:, 0:tok_rows]
    for hop_count in range(reach_blocks):
        carried = shifted(carried, "seq", -1)
        first_row = (hop_count + 1) * tok_rows
        carried = carried + part_pair[:, first_row : first_row + tok_rows]
    key_flat = carried[0].astype(jnp.bfloat16)
    value_flat = carried[1].astype(jnp.bfloat16)

    def project(weight_piece, first_row):
        return lax.dot_general(
            value_flat, weight_piece, (((1,), (1,)), ((), ())), preferred_element_type=jnp.float32
        )

    grad_in = piecewise(value_weight, "fsdp", 0, project, 1).astype(jnp.bfloat16)
    input_local = inputs[0]
    weight_scale = 1.0 / math.sqrt(tok_rows * seq_count * fsdp_count)
    grad_w = (
        lax.psum_scatter(
            lax.dot_general(
                input_local,
                value_flat,
                (((0,), (0,)), ((), ())),
                preferred_element_type=jnp.float32,
            ),
            ("seq", "fsdp"),
            scatter_dimension=0,
            tiled=True,
        )
        * weight_scale
    )
    return (query_back[None], key_flat[None], value_flat[None], grad_in[None], grad_w)


def solution(mesh):
    in_specs = (
        P("fsdp", "seq", None),
        P("fsdp", "seq", None),
        P("fsdp", "seq", None),
        P("fsdp", "seq", None),
        P("fsdp", None),
        P("fsdp", "seq", None),
        P("fsdp", None),
    )
    out_specs = (
        P("fsdp", "seq", None),
        P("fsdp", "seq", None),
        P("fsdp", "seq", None),
        P("fsdp", "seq", None),
        P(("seq", "fsdp"), None),
    )
    return jax.shard_map(local, mesh=mesh, in_specs=in_specs, out_specs=out_specs, check_vma=False)
```

profile of v0, /device:TPU:1, one launch (start us, length us, event | category | flops | bytes accessed | tf_op | source)
XLA Modules:
  0.0 1195.4 jit_solution(13155610029474543549)
XLA Ops:
  15.4 6.1 collective-permute-done
  25.9 6.1 collective-permute-done.1
  36.4 6.1 collective-permute-done.2
  46.9 6.1 collective-permute-done.3
  58.2 6.1 collective-permute-done.4
  69.4 6.1 collective-permute-done.5
  80.7 6.1 collective-permute-done.6
  110.7 140.3 %while.15 = (s32[]{:T(128)}, bf16[8,128,8,128]{1,3,2,0:T(8,128)(2,1)}, f32[8,1152,128]{2,1,0:T(8,128)}, f32[8,1152,128]{2,1,0:T(8,128)}, bf16[8,1152,128]{1,2,0:...) while((s32[]{:T(128)}, ...), condition=%wide.region_6.7_spmd.clone, body=%wide.region_2.6_spmd.clone.sunk | while | flops 1527316608 | bytes 58133164 | solution.py:117
  251.1 8.6 copy.65
  259.7 6.0 stack_reshape.6
  271.1 7.7 copy.66
  278.7 5.9 stack_reshape.7
  293.5 16.5 %collective-permute-done.8 = f32[2,128,1024]{2,1,0:T(8,128)S(1)} collective-permute-done((f32[2,128,1024]{2,1,0:T(8,128)S(1)}, f32[2,128,1024]{2,1,0:T(8,128)S(1)}, u32[]{:S(2)}, u32[]{:S(2)}) %collective-permute-start.8) | collective-permute-done | bytes 1048608 | tf_op jit(solution)/shard_map/ppermute | solution.py:20
  313.3 14.2 %collective-permute-done.9 = f32[2,128,1024]{2,1,0:T(8,128)S(1)} collective-permute-done((f32[2,128,1024]{2,1,0:T(8,128)S(1)}, f32[2,128,1024]{2,1,0:T(8,128)S(1)}, u32[]{:S(2)}, u32[]{:S(2)}) %collective-permute-start.9) | collective-permute-done | bytes 1048608 | tf_op jit(solution)/shard_map/ppermute | solution.py:20
  333.4 11.6 collective-permute-done.10
  348.2 14.2 %collective-permute-done.11 = f32[2,128,1024]{2,1,0:T(8,128)S(1)} collective-permute-done((f32[2,128,1024]{2,1,0:T(8,128)S(1)}, f32[2,128,1024]{2,1,0:T(8,128)S(1)}, u32[]{:S(2)}, u32[]{:S(2)}) %collective-permute-start.11) | collective-permute-done | bytes 1048608 | tf_op jit(solution)/shard_map/ppermute | solution.py:20
  365.7 25.3 %collective-permute-done.12 = f32[2,128,1024]{2,1,0:T(8,128)S(1)} collective-permute-done((f32[2,128,1024]{2,1,0:T(8,128)S(1)}, f32[2,128,1024]{2,1,0:T(8,128)S(1)}, u32[]{:S(2)}, u32[]{:S(2)}) %collective-permute-start.12) | collective-permute-done | bytes 1048608 | tf_op jit(solution)/shard_map/ppermute | solution.py:20
  394.4 37.0 %collective-permute-done.13 = f32[2,128,1024]{2,1,0:T(8,128)S(1)} collective-permute-done((f32[2,128,1024]{2,1,0:T(8,128)S(1)}, f32[2,128,1024]{2,1,0:T(8,128)S(1)}, u32[]{:S(2)}, u32[]{:S(2)}) %collective-permute-start.13) | collective-permute-done | bytes 1048608 | tf_op jit(solution)/shard_map/ppermute | solution.py:20
  434.6 14.6 %collective-permute-done.14 = f32[2,128,1024]{2,1,0:T(8,128)S(1)} collective-permute-done((f32[2,128,1024]{2,1,0:T(8,128)S(1)}, f32[2,128,1024]{2,1,0:T(8,128)S(1)}, u32[]{:S(2)}, u32[]{:S(2)}) %collective-permute-start.14) | collective-permute-done | bytes 1048608 | tf_op jit(solution)/shard_map/ppermute | solution.py:20
  452.5 14.2 %collective-permute-done.15 = f32[2,128,1024]{2,1,0:T(8,128)S(1)} collective-permute-done((f32[2,128,1024]{2,1,0:T(8,128)S(1)}, f32[2,128,1024]{2,1,0:T(8,128)S(1)}, u32[]{:S(2)}, u32[]{:S(2)}) %collective-permute-start.15) | collective-permute-done | bytes 1048608 | tf_op jit(solution)/shard_map/ppermute | solution.py:20
  468.8 9.1 convolution_bitcast_fusion.2
  477.9 17.7 %copy.74 = f32[4096,1024]{1,0:T(8,128)} copy(f32[4096,1024]{0,1:T(8,128)} %convolution_bitcast_fusion.2) | data formatting | bytes 33554432
  503.4 24.5 %all-gather.7.cloned.1.call-done = bf16[2048,1024]{1,0:T(8,128)(2,1)} async-done(((bf16[1024,1024]{1,0:T(8,128)(2,1)}), bf16[2048,1024]{1,0:T(8,128)(2,1)}) %all-gather.7.cloned.1.call-update) | async-done | bytes 4194320 | tf_op jit(solution)/shard_map/all_gather | solution.py:36
  533.7 652.3 %reduce-scatter.4.cloned.1.call-done = f32[32,1024]{1,0:T(8,128)} async-done(((f32[4096,1024]{1,0:T(8,128)}), f32[32,1024]{1,0:T(8,128)}) %reduce-scatter.4.cloned.1.call-update) | async-done | bytes 131088
  (176 shorter events, 257.3 us)
Async XLA Ops:
  8.0 460.8 %copy-start = (bf16[1,128,4096]{2,1,0:T(8,128)(2,1)S(1)}, bf16[1,128,4096]{2,1,0:T(8,128)(2,1)}, u32[]{:S(2)}) copy-start(bf16[1,128,4096]{2,1,0:T(8,128)(2,1)} %param.14) | copy-start | bytes 3145732
  8.0 491.7 %all-gather.5.cloned.1.call-start = ((), (), s32[]{:S(2)}) async-start(), calls=%async_computation.1 | async-start | bytes 6291456 | tf_op jit(solution)/shard_map/all_gather | solution.py:36
  10.4 11.0 collective-permute-start
  21.5 10.5 collective-permute-start.1
  32.0 10.5 collective-permute-start.2
  42.5 10.5 collective-permute-start.3
  53.8 10.5 collective-permute-start.4
  65.1 10.5 collective-permute-start.5
  76.3 10.5 collective-permute-start.6
  86.8 15.8 %collective-permute-start.7 = (bf16[2,128,1024]{1,2,0:T(8,128)(2,1)}, bf16[2,128,1024]{1,2,0:T(8,128)(2,1)}, u32[]{:S(2)}, u32[]{:S(2)}) collective-permute-start(bf16[2,128,1024]{1,2,0:T(8,128)(2,1)} %collective-permute-done.6), channel_id=1, source_target_pairs={{0,2},{2,4},{4,6},{6,8},{8,10},{10,12},{12,14},{14,16},{16,18},{18... | collective-permute-start | bytes 1572872 | tf_op jit(solution)/shard_map/ppermute | solution.py:20
  259.7 11.4 slice-start
  265.7 5.4 slice-start.1
  289.9 40.8 %copy-start.3 = (bf16[2048,1024]{1,0:T(8,128)(2,1)S(1)}, bf16[2048,1024]{1,0:T(8,128)(2,1)}, u32[]{:S(2)}) copy-start(bf16[2048,1024]{1,0:T(8,128)(2,1)} %param.15) | copy-start | bytes 12582916
  291.4 18.6 %collective-permute-start.8 = (f32[2,128,1024]{2,1,0:T(8,128)S(1)}, f32[2,128,1024]{2,1,0:T(8,128)S(1)}, u32[]{:S(2)}, u32[]{:S(2)}) collective-permute-start(f32[2,128,1024]{2,1,0:T(8,128)S(1)} %slice.63), channel_id=1, source_target_pairs={{2,0},{4,2},{6,4},{8,6},{10,8},{12,10},{14,12},{16,14},{18,16},{20... | collective-permute-start | bytes 3145736 | tf_op jit(solution)/shard_map/ppermute | solution.py:20
  311.3 16.1 %collective-permute-start.9 = (f32[2,128,1024]{2,1,0:T(8,128)S(1)}, f32[2,128,1024]{2,1,0:T(8,128)S(1)}, u32[]{:S(2)}, u32[]{:S(2)}) collective-permute-start(f32[2,128,1024]{2,1,0:T(8,128)S(1)} %slice_add_fusion.7), channel_id=1, source_target_pairs={{2,0},{4,2},{6,4},{8,6},{10,8},{12,10},{14,12},{16,14},{18,16},{20... | collective-permute-start | bytes 3145736 | tf_op jit(solution)/shard_map/ppermute | solution.py:20
  328.8 16.1 %collective-permute-start.10 = (f32[2,128,1024]{2,1,0:T(8,128)S(1)}, f32[2,128,1024]{2,1,0:T(8,128)S(1)}, u32[]{:S(2)}, u32[]{:S(2)}) collective-permute-start(f32[2,128,1024]{2,1,0:T(8,128)S(1)} %slice_add_fusion.6), channel_id=1, source_target_pairs={{2,0},{4,2},{6,4},{8,6},{10,8},{12,10},{14,12},{16,14},{18,16},{20... | collective-permute-start | bytes 3145736 | tf_op jit(solution)/shard_map/ppermute | solution.py:20
  333.3 194.6 %all-gather.7.cloned.1.call-start = ((), (), s32[]{:S(2)}) async-start(), calls=%async_computation.2 | async-start | bytes 6291456 | tf_op jit(solution)/shard_map/all_gather | solution.py:36
  346.3 16.1 %collective-permute-start.11 = (f32[2,128,1024]{2,1,0:T(8,128)S(1)}, f32[2,128,1024]{2,1,0:T(8,128)S(1)}, u32[]{:S(2)}, u32[]{:S(2)}) collective-permute-start(f32[2,128,1024]{2,1,0:T(8,128)S(1)} %slice_add_fusion.5), channel_id=1, source_target_pairs={{2,0},{4,2},{6,4},{8,6},{10,8},{12,10},{14,12},{16,14},{18,16},{20... | collective-permute-start | bytes 3145736 | tf_op jit(solution)/shard_map/ppermute | solution.py:20
  363.8 27.2 %collective-permute-start.12 = (f32[2,128,1024]{2,1,0:T(8,128)S(1)}, f32[2,128,1024]{2,1,0:T(8,128)S(1)}, u32[]{:S(2)}, u32[]{:S(2)}) collective-permute-start(f32[2,128,1024]{2,1,0:T(8,128)S(1)} %slice_add_fusion.4), channel_id=1, source_target_pairs={{2,0},{4,2},{6,4},{8,6},{10,8},{12,10},{14,12},{16,14},{18,16},{20... | collective-permute-start | bytes 3145736 | tf_op jit(solution)/shard_map/ppermute | solution.py:20
  392.4 39.0 %collective-permute-start.13 = (f32[2,128,1024]{2,1,0:T(8,128)S(1)}, f32[2,128,1024]{2,1,0:T(8,128)S(1)}, u32[]{:S(2)}, u32[]{:S(2)}) collective-permute-start(f32[2,128,1024]{2,1,0:T(8,128)S(1)} %slice_add_fusion.3), channel_id=1, source_target_pairs={{2,0},{4,2},{6,4},{8,6},{10,8},{12,10},{14,12},{16,14},{18,16},{20... | collective-permute-start | bytes 3145736 | tf_op jit(solution)/shard_map/ppermute | solution.py:20
  394.3 791.7 %reduce-scatter.4.cloned.1.call-start = ((), (), s32[]{:S(2)}) async-start(), calls=%async_computation.3 | async-start | bytes 16908288
  432.7 16.5 %collective-permute-start.14 = (f32[2,128,1024]{2,1,0:T(8,128)S(1)}, f32[2,128,1024]{2,1,0:T(8,128)S(1)}, u32[]{:S(2)}, u32[]{:S(2)}) collective-permute-start(f32[2,128,1024]{2,1,0:T(8,128)S(1)} %slice_add_fusion.2), channel_id=1, source_target_pairs={{2,0},{4,2},{6,4},{8,6},{10,8},{12,10},{14,12},{16,14},{18,16},{20... | collective-permute-start | bytes 3145736 | tf_op jit(solution)/shard_map/ppermute | solution.py:20
  450.6 16.1 %collective-permute-start.15 = (f32[2,128,1024]{2,1,0:T(8,128)S(1)}, f32[2,128,1024]{2,1,0:T(8,128)S(1)}, u32[]{:S(2)}, u32[]{:S(2)}) collective-permute-start(f32[2,128,1024]{2,1,0:T(8,128)S(1)} %slice_add_fusion.1), channel_id=1, source_target_pairs={{2,0},{4,2},{6,4},{8,6},{10,8},{12,10},{14,12},{16,14},{18,16},{20... | collective-permute-start | bytes 3145736 | tf_op jit(solution)/shard_map/ppermute | solution.py:20
  468.8 59.1 %copy-start.2 = (bf16[1,128,1024]{2,1,0:T(8,128)(2,1)}, bf16[1,128,1024]{2,1,0:T(8,128)(2,1)S(1)}, u32[]{:S(2)}) copy-start(bf16[1,128,1024]{2,1,0:T(8,128)(2,1)S(1)} %get-tuple-element.167) | copy-start | bytes 786436
  (19 other events, 65.1 us)
Sparse Core Ops, SparseCore 0:
  333.4 132.7 all-gather.4
  467.9 59.9 all-gather.6
Sparse Core Ops, SparseCore 1:
  495.7 690.2 reduce-scatter.3
where the time goes:
time: 1200 us
  waiting for transfers between devices  867 us (72%)
  matrix products  140 us (12%)
  local copies, waits for them, and re-layouts  95.7 us (8%)
  starting transfers between devices  51.3 us (4%)
  other arithmetic  24.8 us (2%)
  between operations  15.8 us (1%)
    unnamed x4, waiting for transfers between devices  652 us
    ppermute x16, waiting for transfers between devices, shifted(): return lax.ppermute(value, axis, pairs)  190 us
    ppermute x16, starting transfers between devices, shifted(): return lax.ppermute(value, axis, pairs)  51.2 us
    sub x8, matrix products, group_backward(): weights = jnp.where(allowed[None], jnp.exp(scores - row_max), 0.0)  45.5 us
    unnamed x33, local copies, waits for them, and re-layouts  45.4 us
    dot_general x8, matrix products, group_backward(): jnp.einsum('qhd,kd->hqk', grad_group, value_slab, preferred_element_type=...  27.7 us
    all_gather x2, waiting for transfers between devices, piecewise(): done.append(jax.vmap(apply)(lax.all_gather(piece, axis), starts))  24.5 us
  transfers between devices with their start and end apart: 19, of which 17 were waited for; matrix products, arithmetic and copies ran while one was open for 5% of the time, Pallas kernels for 0%

commit v1 on v0

v1 whole, which is shorter than its diff:
```python
import math

import jax
import jax.numpy as jnp
from jax import lax
from jax.experimental import pallas as pl
from jax.experimental.pallas import tpu as pltpu
from jax.sharding import PartitionSpec as P

D = 128
T = 256
W = 1280
HALF = 4
HB = 4
SCALE = 1.0 / math.sqrt(D)
EXP2 = math.log2(math.e) * SCALE
NT = (((1,), (1,)), ((), ()))
f32, bf16 = jnp.float32, jnp.bfloat16
MESH = pl.DeviceIdType.MESH
ANY = pl.BlockSpec(memory_space=pl.ANY)
VMEM = pl.BlockSpec(memory_space=pltpu.VMEM)


def position():
    p, f = lax.axis_index("seq"), lax.axis_index("fsdp")
    return p, f, p // 16, p // 4 % 4, p // 2 % 2, p % 2


def wrapped(p, by):
    return lax.rem(p + by + 64, 64)


def along_x(p, dx):
    return lax.rem(p + 16 * dx, 64)


def along_y(p, y, dy):
    return p - 4 * y + 4 * lax.rem(y + dy, 4)


def greet(devices):
    barrier = pltpu.get_barrier_semaphore()
    for device in devices:
        pl.semaphore_signal(barrier, inc=1, device_id=device, device_id_type=MESH)
    pl.semaphore_wait(barrier, len(devices))


def rows_of(index, size=T):
    return pl.ds(pl.multiple_of(index * size, size), size)


def gather_kernel(
    q_ref, do_ref, k_ref, v_ref, in_ref, w_ref, qx_ref, dox_ref, slab_ref, inx_ref, wx_ref, send, recv, near
):
    p, f, x, y, zl, k = position()
    sib = (p + 1 - 2 * k, f)
    zdev = (p + 2 - 4 * zl, f)
    up, down = (wrapped(p, 4), f), (wrapped(p, -4), f)
    fdev = (p, 1 - f)
    xs = [(along_x(p, dx), f) for dx in (1, 2, 3)]
    greet([sib, zdev, up, down, fdev] + xs)
    count = [0]

    def remote(src, dst, device):
        i = count[0]
        count[0] += 1
        copy = pltpu.make_async_remote_copy(
            src_ref=src, dst_ref=dst, send_sem=send.at[i], recv_sem=recv.at[i], device_id=device, device_id_type=MESH
        )
        copy.start()
        return copy

    nears = []

    def local(src, dst):
        copy = pltpu.make_async_copy(src, dst, near.at[len(nears)])
        copy.start()
        nears.append(copy)
        return copy

    own = rows_of(k, 128)
    mine4, theirs4 = rows_of(k, 4096), rows_of(1 - k, 4096)
    mine, theirs = rows_of(k, 512), rows_of(1 - k, 512)
    at = pl.ds(pl.multiple_of(1024 + k * 128, 128), 128)
    kv = [
        remote(k_ref.at[:, theirs], slab_ref.at[0, at, :], sib),
        remote(v_ref.at[:, theirs], slab_ref.at[1, at, :], sib),
    ]
    kv_near = [local(k_ref.at[:, mine], slab_ref.at[0, at, :]), local(v_ref.at[:, mine], slab_ref.at[1, at, :])]
    quarter = pl.ds(pl.multiple_of(k * 1024 + x * 256, 256), 256)
    w0 = remote(w_ref.at[quarter, :], wx_ref.at[rows_of(x), :], fdev)
    ins = []
    for dx in (1, 2, 3):
        cols = rows_of(lax.rem(x + dx, 4), 1024)
        ins.append(remote(in_ref.at[:, cols], inx_ref.at[x, own, :], xs[dx - 1]))
    qs = [
        remote(q_ref.at[:, theirs4], qx_ref.at[own, :], sib),
        remote(do_ref.at[:, theirs4], dox_ref.at[own, :], sib),
        remote(in_ref.at[:, rows_of(x, 1024)], inx_ref.at[x, own, :], sib),
    ]
    local(q_ref.at[:, mine4], qx_ref.at[own, :])
    local(do_ref.at[:, mine4], dox_ref.at[own, :])
    local(in_ref.at[:, rows_of(x, 1024)], inx_ref.at[x, own, :])

    def block(index):
        return slab_ref.at[:, rows_of(index), :]

    for c in kv:
        c.wait_recv()
    for c in kv_near:
        c.wait()
    y0 = remote(block(4), block(2), up)
    y0.wait_recv()
    y1 = remote(block(2), block(0), up)
    z0 = remote(block(4 - 2 * zl), block(3), zdev)
    w0.wait_recv()
    ws = [remote(wx_ref.at[rows_of(x), :], wx_ref.at[rows_of(x), :], xs[dx - 1]) for dx in (1, 2, 3)]
    y1.wait_recv()
    z1 = remote(block(2 - 2 * zl), block(1), zdev)
    shared = []
    for dx in (1, 2, 3):
        ins[dx - 1].wait_recv()
        piece = inx_ref.at[lax.rem(x + 4 - dx, 4), own, :]
        shared.append(remote(piece, piece, sib))
    for c in nears[2:]:
        c.wait()
    for c in qs + ws + shared + [z0, z1]:
        c.wait_recv()
    for c in kv + [w0] + ins + qs + [y0, y1, z0, z1] + ws + shared:
        c.wait_send()


def gather(queries, out_grad, keys, values, inputs, weight):
    messages = 20
    return pl.pallas_call(
        gather_kernel,
        out_shape=[
            jax.ShapeDtypeStruct((T, 4096), bf16),
            jax.ShapeDtypeStruct((T, 4096), bf16),
            jax.ShapeDtypeStruct((2, W, 512), bf16),
            jax.ShapeDtypeStruct((4, T, 1024), bf16),
            jax.ShapeDtypeStruct((1024, 1024), bf16),
        ],
        in_specs=[ANY] * 6,
        out_specs=[ANY] * 5,
        scratch_shapes=[
            pltpu.SemaphoreType.DMA((messages,)),
            pltpu.SemaphoreType.DMA((messages,)),
            pltpu.SemaphoreType.DMA((5,)),
        ],
        compiler_params=pltpu.CompilerParams(collective_id=0, has_side_effects=True),
        name="gather",
    )(queries, out_grad, keys, values, inputs, weight)


def attend(q, do, k_ref, v_ref, kt_ref, bias_ref, s_ref, dp_ref, p_ref, ds_ref):
    s_ref[...] = lax.dot_general(k_ref[...], q, NT, preferred_element_type=f32)
    dp_ref[...] = lax.dot_general(v_ref[...], do, NT, preferred_element_type=f32)
    step = 128
    top = None
    for i in range(0, W, step):
        s = s_ref[i : i + step, :] + bias_ref[i : i + step, :]
        t = jnp.max(s.reshape(step // 8, 8, T), axis=0)
        top = t if top is None else jnp.maximum(top, t)
    top = jnp.max(top, axis=0, keepdims=True)
    total = delta = 0.0
    for i in range(0, W, step):
        e = jnp.exp2((s_ref[i : i + step, :] + bias_ref[i : i + step, :] - top) * EXP2)
        p_ref[i : i + step, :] = e.astype(bf16)
        total += jnp.sum(e.reshape(step // 8, 8, T), axis=0)
        delta += jnp.sum((e * dp_ref[i : i + step, :]).reshape(step // 8, 8, T), axis=0)
    inverse = 1.0 / jnp.sum(total, axis=0, keepdims=True)
    delta = jnp.sum(delta, axis=0, keepdims=True) * inverse
    for i in range(0, W, step):
        e = p_ref[i : i + step, :].astype(f32)
        ds_ref[i : i + step, :] = (e * (dp_ref[i : i + step, :] - delta)).astype(bf16)
    dq = jnp.dot(kt_ref[...], ds_ref[...], preferred_element_type=f32) * (inverse * SCALE)
    return dq.T, jnp.broadcast_to(inverse, (D, T)).T


def attention_kernel(
    key_doc, query_doc, q_ref, do_ref, k_ref, v_ref, dq_ref, dkv_ref, kt_ref, bias_ref, *scratch
):
    g, j = pl.program_id(0), pl.program_id(1)

    @pl.when((g == 0) & (j == 0))
    def _():
        key_at = lax.broadcasted_iota(jnp.int32, (W, T), 0)
        query_at = lax.broadcasted_iota(jnp.int32, (W, T), 1)
        allowed = (key_doc[...] == query_doc[...]) & (key_at <= query_at + (W - T))
        bias_ref[...] = jnp.where(allowed, 0.0, -1e30).astype(f32)

    @pl.when(j == 0)
    def _():
        kt_ref[...] = k_ref[...].T
        dkv_ref[...] = jnp.zeros_like(dkv_ref)

    for a in range(HB):
        cols = slice(a * D, (a + 1) * D)
        q, do = q_ref[:, cols], do_ref[:, cols]
        s_ref, dp_ref, p_ref, ds_ref = scratch[4 * a : 4 * a + 4]
        dq, inverse = attend(q, do, k_ref, v_ref, kt_ref, bias_ref, s_ref, dp_ref, p_ref, ds_ref)
        dq_ref[:, cols] = dq.astype(bf16)
        dkv_ref[0, 0] += jnp.dot(ds_ref[...], (q * inverse).astype(bf16), preferred_element_type=f32)
        dkv_ref[0, 1] += jnp.dot(p_ref[...], (do * inverse).astype(bf16), preferred_element_type=f32)


def attention(key_doc, query_doc, q, do, slab):
    n = 8 // HB
    scratch = []
    for _ in range(HB):
        scratch += [pltpu.VMEM((W, T), t) for t in (f32, f32, bf16, bf16)]
    heads = pl.BlockSpec((T, HB * D), lambda g, j: (0, g * n + j))
    return pl.pallas_call(
        attention_kernel,
        grid=(HALF, n),
        in_specs=[
            pl.BlockSpec((W, 1), lambda g, j: (0, 0)),
            pl.BlockSpec((1, T), lambda g, j: (0, 0)),
            heads,
            heads,
            pl.BlockSpec((None, W, D), lambda g, j: (0, 0, g)),
            pl.BlockSpec((None, W, D), lambda g, j: (1, 0, g)),
        ],
        out_specs=[heads, pl.BlockSpec((1, 2, W, D), lambda g, j: (g, 0, 0, 0))],
        out_shape=[jax.ShapeDtypeStruct((T, 4096), bf16), jax.ShapeDtypeStruct((HALF, 2, W, D), f32)],
        scratch_shapes=[pltpu.VMEM((D, W), bf16), pltpu.VMEM((W, T), f32)] + scratch,
        compiler_params=pltpu.CompilerParams(vmem_limit_bytes=50 * 2**20),
        name="attention",
    )(key_doc, query_doc, q, do, slab, slab)


def reduce_kernel(
    dkv_ref, dq_ref, inx_ref, w_ref, wx_ref,
    gq_ref, gk_ref, gv_ref, gi_ref, gw_ref,
    zsend, zrecv, ysend, yrecv, gkcat, gvcat, gx, wk, gibuf, gw_send, gw_recv, gw_own, zst, rz, last, fin, last_recv,
    send, recv, near,
):
    p, f, x, y, zl, k = position()
    sib = (p + 1 - 2 * k, f)
    zp = p + 2 - 4 * zl
    zdev = (zp, f)
    up, down = (wrapped(p, 4), f), (wrapped(p, -4), f)
    xs = [(along_x(p, dx), f) for dx in (1, 2, 3)]
    ys = [(along_y(p, y, dy), f) for dy in (1, 2, 3)]
    zs = [(p, 1 - f), (zp, f), (zp, 1 - f)]
    greet([sib, up, down] + xs + ys + zs)
    sent = []

    def remote(src, dst, device):
        i = len(sent)
        copy = pltpu.make_async_remote_copy(
            src_ref=src, dst_ref=dst, send_sem=send.at[i], recv_sem=recv.at[i], device_id=device, device_id_type=MESH
        )
        copy.start()
        sent.append(copy)
        return copy

    mine4 = rows_of(k, 4096)
    own, other = rows_of(k, 128), rows_of(1 - k, 128)
    near_gq = pltpu.make_async_copy(dq_ref.at[own, :], gq_ref.at[:, mine4], near.at[0])
    near_gq.start()
    near_w = pltpu.make_async_copy(w_ref.at[rows_of(k, 1024), :], wk, near.at[1])
    near_w.start()
    last_waits = [remote(dq_ref.at[other, :], gq_ref.at[:, mine4], sib)]

    def block(index):
        return slice(index * T, (index + 1) * T)

    first = []
    for g in range(HALF):
        for a, index in enumerate((3, 1)):
            zsend[g, a] = dkv_ref[g, :, block(index), :].astype(bf16)
        first.append(remote(zsend.at[g], zrecv.at[g], zdev))
    upper = zl == 1
    second = []
    for g in range(HALF):
        first[g].wait_recv()
        r0, r1 = zrecv[g, 0].astype(f32), zrecv[g, 1].astype(f32)
        ysend[g, 0] = (dkv_ref[g, :, block(0), :] + jnp.where(upper, r1, 0.0)).astype(bf16)
        second.append(remote(ysend.at[g, 0], yrecv.at[g, 0], down))
    third = []
    for g in range(HALF):
        second[g].wait_recv()
        r0, r1 = zrecv[g, 0].astype(f32), zrecv[g, 1].astype(f32)
        part = dkv_ref[g, :, block(2), :] + jnp.where(upper, r0, r1) + yrecv[g, 0].astype(f32)
        ysend[g, 1] = part.astype(bf16)
        third.append(remote(ysend.at[g, 1], yrecv.at[g, 1], down))
    for g in range(HALF):
        third[g].wait_recv()
        r0 = zrecv[g, 0].astype(f32)
        part = dkv_ref[g, :, block(4), :] + jnp.where(upper, 0.0, r0) + yrecv[g, 1].astype(f32)
        cols = pl.ds(pl.multiple_of((HALF * k + g) * D, D), D)
        gkcat[:, cols] = (part[0] * SCALE).astype(bf16)
        grad = part[1].astype(bf16)
        gvcat[:, cols] = grad
        gx[g * D : (g + 1) * D, rows_of(x)] = part[1].T.astype(bf16)
    mine = rows_of(k, 512)
    across = [remote(c.at[:, mine], c.at[:, mine], sib) for c in (gvcat, gkcat)]
    gxs = [remote(gx.at[:, rows_of(x)], gx.at[:, rows_of(x)], xs[dx - 1]) for dx in (1, 2, 3)]
    for c in across:
        c.wait_recv()
    gk_ref[...] = gkcat[own, :]
    gv_ref[...] = gvcat[own, :]
    near_w.wait()
    outs = []
    for j, w in enumerate((wk, wx_ref)):
        cols = rows_of((f if j == 0 else 1 - f) * 2 + k, 1024)
        for i in range(0, 1024, 256):
            gibuf[j, :, i : i + 256] = lax.dot_general(
                gvcat[...], w[i : i + 256, :], NT, preferred_element_type=f32
            ).astype(bf16)
        here = pltpu.make_async_copy(gibuf.at[j, own, :], gi_ref.at[:, cols], near.at[2 + j])
        here.start()
        outs.append(here)
        last_waits.append(remote(gibuf.at[j, other, :], gi_ref.at[:, cols], sib))
    for c in gxs:
        c.wait_recv()
    gws = []
    for dy in (1, 2, 3, 0):
        cols = rows_of(lax.rem(y + dy, 4))
        part = jnp.dot(gx[...], inx_ref[:, cols], preferred_element_type=f32)
        if dy:
            gw_send[dy - 1] = part.astype(bf16)
            gws.append(remote(gw_send.at[dy - 1], gw_recv.at[dy - 1], ys[dy - 1]))
        else:
            gw_own[...] = part
    for c in gws:
        c.wait_recv()
    part = (gw_own[...] + gw_recv[0].astype(f32) + gw_recv[1].astype(f32) + gw_recv[2].astype(f32)).T
    part = part.reshape(2, 2, 2, 32, 512)
    for a in range(2):
        for c in range(2):
            zst[a, c] = part[a, :, c]
    rzs = []
    for j, device in enumerate(zs):
        to_z, to_f = (zl, 1 - zl, 1 - zl)[j], (1 - f, f, 1 - f)[j]
        last[j] = zst[to_z, to_f].astype(bf16)
        rzs.append(remote(last.at[j], rz.at[j], device))
    for c in rzs:
        c.wait_recv()
    done = zst[zl, f] + rz[0].astype(f32) + rz[1].astype(f32) + rz[2].astype(f32)
    fin[...] = done * (1.0 / math.sqrt(2 * 8192))
    final = remote(fin.at[1 - k], last_recv, sib)
    gw_ref[:, mine] = fin[k]
    final.wait_recv()
    gw_ref[:, rows_of(1 - k, 512)] = last_recv[...]
    near_gq.wait()
    for c in outs:
        c.wait()
    for c in last_waits:
        c.wait_recv()
    for c in sent:
        c.wait_send()


def reduce(dkv, dq, inx, weight, wx):
    messages = 27
    pair = (2, T, D)
    return pl.pallas_call(
        reduce_kernel,
        out_shape=[
            jax.ShapeDtypeStruct((128, 8192), bf16),
            jax.ShapeDtypeStruct((128, 1024), bf16),
            jax.ShapeDtypeStruct((128, 1024), bf16),
            jax.ShapeDtypeStruct((128, 4096), bf16),
            jax.ShapeDtypeStruct((32, 1024), f32),
        ],
        in_specs=[VMEM, ANY, VMEM, ANY, VMEM],
        out_specs=[ANY, VMEM, VMEM, ANY, VMEM],
        scratch_shapes=[
            pltpu.VMEM((HALF, 2) + pair, bf16),
            pltpu.VMEM((HALF, 2) + pair, bf16),
            pltpu.VMEM((HALF, 2) + pair, bf16),
            pltpu.VMEM((HALF, 2) + pair, bf16),
            pltpu.VMEM((T, 1024), bf16),
            pltpu.VMEM((T, 1024), bf16),
            pltpu.VMEM((512, 1024), bf16),
            pltpu.VMEM((1024, 1024), bf16),
            pltpu.VMEM((2, T, 1024), bf16),
            pltpu.VMEM((3, 512, T), bf16),
            pltpu.VMEM((3, 512, T), bf16),
            pltpu.VMEM((512, T), f32),
            pltpu.VMEM((2, 2, 2, 32, 512), f32),
            pltpu.VMEM((3, 2, 32, 512), bf16),
            pltpu.VMEM((3, 2, 32, 512), bf16),
            pltpu.VMEM((2, 32, 512), f32),
            pltpu.VMEM((32, 512), f32),
            pltpu.SemaphoreType.DMA((messages,)),
            pltpu.SemaphoreType.DMA((messages,)),
            pltpu.SemaphoreType.DMA((4,)),
        ],
        compiler_params=pltpu.CompilerParams(
            collective_id=1, has_side_effects=True, vmem_limit_bytes=50 * 2**20
        ),
        name="reduce",
    )(dkv, dq, inx, weight, wx)


def documents(lengths):
    chip = lax.axis_index("seq") // 2
    entry = jnp.arange(lengths.shape[0])
    bounds = jnp.sum(jnp.where(entry[None, :] <= entry[:, None], lengths[None, :], 0), axis=1)
    at = chip * T - (W - T) + jnp.arange(W, dtype=jnp.int32)
    ids = jnp.sum((at[:, None] >= bounds[None, :]).astype(jnp.int32), axis=1)
    return jnp.where(at < 0, -1, ids)


def local(queries, keys, values, out_grad, doc_lengths, inputs, value_weight):
    ids = documents(doc_lengths[0])
    qx, dox, slab, inx, wx = gather(queries[0], out_grad[0], keys[0], values[0], inputs[0], value_weight)
    dq, dkv = attention(ids[:, None], ids[None, W - T :], qx, dox, slab)
    gq, gk, gv, gi, gw = reduce(dkv, dq, inx.reshape(1024, 1024), value_weight, wx)
    return gq[None], gk[None], gv[None], gi[None], gw


def solution(mesh):
    tokens = P("fsdp", "seq", None)
    in_specs = (tokens, tokens, tokens, tokens, P("fsdp", None), tokens, P("fsdp", None))
    out_specs = (tokens, tokens, tokens, tokens, P(("seq", "fsdp"), None))
    return jax.shard_map(local, mesh=mesh, in_specs=in_specs, out_specs=out_specs, check_vma=False)
```

time: 1200 us -> 222 us (0.18)
  waiting for transfers between devices: 867 us -> 0 us
  Pallas kernels: 0 us -> 214 us
  matrix products: 140 us -> 0 us
  local copies, waits for them, and re-layouts: 95.7 us -> 5.67 us
  starting transfers between devices: 51.3 us -> 0 us
  other arithmetic: 24.8 us -> 1.12 us
  between operations: 15.8 us -> 0.7 us
    unnamed x4 -> x0, waiting for transfers between devices: 652 us -> none
    pallas_call x0 -> x3, Pallas kernels: none -> 214 us  [the longest x1 86.8 us: gather(): pl.pallas_call(gather_kernel, out_shape=[jax.ShapeDtypeStruct((T, 4096),...]
    ppermute x16 -> x0, waiting for transfers between devices: 190 us -> none  [shifted(): return lax.ppermute(value, axis, pairs)]
    dot_general x35 -> x0, matrix products: 95 us -> none  [the longest x8 27.7 us: group_backward(): jnp.einsum('qhd,kd->hqk', grad_group, value_slab, preferred_element_type=...]
    ppermute x16 -> x0, starting transfers between devices: 51.2 us -> none  [shifted(): return lax.ppermute(value, axis, pairs)]
    sub x8 -> x0, matrix products: 45.5 us -> none  [group_backward(): weights = jnp.where(allowed[None], jnp.exp(scores - row_max), 0.0)]
    unnamed x33 -> x7, local copies, waits for them, and re-layouts: 45.4 us -> 5.67 us
    all_gather x2 -> x0, waiting for transfers between devices: 24.5 us -> none  [piecewise(): done.append(jax.vmap(apply)(lax.all_gather(piece, axis), starts))]
  transfers between devices with their start and end apart: 19 -> 0, of which waited for: 17 -> 0; matrix products, arithmetic and copies ran while one was open for 5% -> 0% of each run, Pallas kernels for 0% -> 0%
where the time goes in v1:
time: 222 us
  Pallas kernels  214 us (96%)
  local copies, waits for them, and re-layouts  5.67 us (3%)
    pallas_call x1, Pallas kernels, gather(): pl.pallas_call(gather_kernel, out_shape=[jax.ShapeDtypeStruct((T, 4096),...  86.8 us
    pallas_call x1, Pallas kernels, reduce(): pl.pallas_call(reduce_kernel, out_shape=[jax.ShapeDtypeStruct((128, 8192)...  78.2 us
    pallas_call x1, Pallas kernels, attention(): pl.pallas_call(attention_kernel, grid=(HALF, n), in_specs=[pl.BlockSpec((...  49.2 us
    unnamed x7, local copies, waits for them, and re-layouts  5.67 us

profile of v1, /device:TPU:1, one launch (start us, length us, event | category | flops | bytes accessed | tf_op | source)
XLA Modules:
  0.0 221.7 jit_solution(4283827561469809260)
XLA Ops:
  0.6 0.8 select_reduce_fusion
  1.4 0.1 convert_reduce_fusion
  1.6 0.2 reshape_select_fusion.key_doc
  1.8 86.8 %gather.1 = (bf16[256,4096]{1,0:T(8,128)(2,1)}, bf16[256,4096]{1,0:T(8,128)(2,1)}, bf16[2,1280,512]{2,1,0:T(8,128)(2,1)}, bf16[4,256,1024]{2,1,0:T(8,128)(2,1)}, bf16[1024,1024]{1,0:T(8,128)(2,1)}) custom-call(bf16[128,8192]{1,0:T(8,128)(2,1)} %bitcast.17, bf16[128,8192]{1,0:T(8,128)(2,1)} %bitcast.18, bf16[128,1024]{1,0:T(8,128)(2,1)} %bitcast.21, ...), custom_call_target="tpu_custom_call" | custom-call | tf_op jit(solution)/shard_map/gather/pallas_call | solution.py:135
  88.7 49.2 %attention.1 = (bf16[256,4096]{1,0:T(8,128)(2,1)S(1)}, f32[4,2,1280,128]{3,2,1,0:T(8,128)}) custom-call(s32[1280,1]{1,0:T(8,128)S(1)} %reshape_select_fusion.key_doc, s32[1,256]{1,0:T(1,128)S(1)} %bitcast.16, bf16[256,4096]{1,0:T(8,128)(2,1)} %get-tuple-element.17.q_ref, bf16[256,4096]{1,0:T(8,128)(2,1)} %get-tuple-element.18.do_ref, ...), custom_call_target="tpu_custom_call" | custom-call | tf_op jit(solution)/shard_map/attention/pallas_call | solution.py:214
  137.8 0.0 copy-start
  137.8 1.3 copy-done
  139.1 78.2 %reduce.1 = (bf16[128,8192]{1,0:T(8,128)(2,1)S(1)}, bf16[128,1024]{1,0:T(8,128)(2,1)S(1)}, bf16[128,1024]{1,0:T(8,128)(2,1)S(1)}, bf16[128,4096]{1,0:T(8,128)(2,1)S(1)}, f32[32,1024]{1,0:T(8,128)S(1)}) custom-call(f32[4,2,1280,128]{3,2,1,0:T(8,128)} %get-tuple-element.20.dkv_ref, bf16[256,4096]{1,0:T(8,128)(2,1)} %copy-done, bf16[1024,1024]{1,0:T(8,128)(2,1)} %bitcast.19, ...), custom_call_target="tpu_custom_call" | custom-call | tf_op jit(solution)/shard_map/reduce/pallas_call | solution.py:360
  217.3 1.3 copy.19
  218.6 0.7 copy.20
  219.3 0.7 copy.21
  220.0 1.0 copy.22
  221.0 0.7 copy.23
  (2 shorter events, 0.0 us)
Async XLA Ops:
  137.8 1.3 copy-start

commit v2 on v0

v2 whole, which is shorter than its diff:
```python
import math

import jax
import jax.numpy as jnp
from jax import lax
from jax.experimental import pallas as pl
from jax.experimental.pallas import tpu as pltpu
from jax.sharding import PartitionSpec as P

D = 128
T = 256
W = 1280
HALF = 4
HB = 4
MESSAGES = 109
SCALE = 1.0 / math.sqrt(D)
EXP2 = math.log2(math.e) * SCALE
NT = (((1,), (1,)), ((), ()))
f32, bf16 = jnp.float32, jnp.bfloat16
MESH = pl.DeviceIdType.MESH
ANY = pl.BlockSpec(memory_space=pl.ANY)
VMEM = pl.BlockSpec(memory_space=pltpu.VMEM)


def position():
    p, f = lax.axis_index("seq"), lax.axis_index("fsdp")
    return p, f, p // 16, p // 4 % 4, p // 2 % 2, p % 2


def wrapped(p, by):
    return lax.rem(p + by + 64, 64)


def along_x(p, dx):
    return lax.rem(p + 16 * dx, 64)


def along_y(p, y, dy):
    return p - 4 * y + 4 * lax.rem(y + dy, 4)


def greet(devices):
    barrier = pltpu.get_barrier_semaphore()
    for device in devices:
        pl.semaphore_signal(barrier, inc=1, device_id=device, device_id_type=MESH)
    pl.semaphore_wait(barrier, len(devices))


def rows_of(index, size=T):
    return pl.ds(pl.multiple_of(index * size, size), size)


def attend(q, do, k_ref, v_ref, kt_ref, bias_ref, s_ref, dp_ref, p_ref, ds_ref):
    s_ref[...] = lax.dot_general(k_ref[...], q, NT, preferred_element_type=f32)
    dp_ref[...] = lax.dot_general(v_ref[...], do, NT, preferred_element_type=f32)
    step = 128
    top = None
    for i in range(0, W, step):
        s = s_ref[i : i + step, :] + bias_ref[i : i + step, :]
        t = jnp.max(s.reshape(step // 8, 8, T), axis=0)
        top = t if top is None else jnp.maximum(top, t)
    top = jnp.max(top, axis=0, keepdims=True)
    total = delta = 0.0
    for i in range(0, W, step):
        e = jnp.exp2((s_ref[i : i + step, :] + bias_ref[i : i + step, :] - top) * EXP2)
        p_ref[i : i + step, :] = e.astype(bf16)
        total += jnp.sum(e.reshape(step // 8, 8, T), axis=0)
        delta += jnp.sum((e * dp_ref[i : i + step, :]).reshape(step // 8, 8, T), axis=0)
    inverse = 1.0 / jnp.sum(total, axis=0, keepdims=True)
    delta = jnp.sum(delta, axis=0, keepdims=True) * inverse
    for i in range(0, W, step):
        e = p_ref[i : i + step, :].astype(f32)
        ds_ref[i : i + step, :] = (e * (dp_ref[i : i + step, :] - delta)).astype(bf16)
    dq = jnp.dot(kt_ref[...], ds_ref[...], preferred_element_type=f32) * (inverse * SCALE)
    return dq.T, jnp.broadcast_to(inverse, (D, T)).T


def kernel(
    key_doc, query_doc, q_in, do_in, k_in, v_in, in_ref, w_ref,
    gq_ref, gk_ref, gv_ref, gi_ref, gw_ref,
    qx, dox, slab, inx, wk, wx, dq, acc, kt, bias,
    zsend, zrecv, ysend, yrecv, cat, gx, gibuf, gw_send, gw_recv, gw_own, zst, last, rz, fin, last_recv,
    send, recv, near, *scratch,
):
    p, f, x, y, zl, k = position()
    sib = (p + 1 - 2 * k, f)
    zp = p + 2 - 4 * zl
    zdev = (zp, f)
    up, down = (wrapped(p, 4), f), (wrapped(p, -4), f)
    xs = [(along_x(p, dx), f) for dx in (1, 2, 3)]
    ys = [(along_y(p, y, dy), f) for dy in (1, 2, 3)]
    zs = [(p, 1 - f), (zp, f), (zp, 1 - f)]
    every, nears = [], []

    def remote(src, dst, device):
        i = len(every)
        copy = pltpu.make_async_remote_copy(
            src_ref=src, dst_ref=dst, send_sem=send.at[i], recv_sem=recv.at[i], device_id=device, device_id_type=MESH
        )
        every.append(copy)
        return copy

    def local(src, dst):
        copy = pltpu.make_async_copy(src, dst, near.at[len(nears)])
        nears.append(copy)
        return copy

    own, other = rows_of(k, 128), rows_of(1 - k, 128)
    here = pl.ds(pl.multiple_of(1024 + k * 128, 128), 128)

    def column(core, g, size):
        return rows_of(core * HALF + g, size)

    def window(g, index):
        return slab.at[g, :, rows_of(index), :]

    kv, kv_near, qs, q_near = [], [], [], []
    for g in range(HALF):
        kv.append([remote(a.at[:, column(1 - k, g, D)], slab.at[g, i, here, :], sib) for i, a in enumerate((k_in, v_in))])
        kv_near.append([local(a.at[:, column(k, g, D)], slab.at[g, i, here, :]) for i, a in enumerate((k_in, v_in))])
        cols = pl.ds(g * 1024, 1024)
        pairs = ((q_in, qx), (do_in, dox))
        qs.append([remote(a.at[:, column(1 - k, g, 1024)], b.at[own, cols], sib) for a, b in pairs])
        q_near.append([local(a.at[:, column(k, g, 1024)], b.at[own, cols]) for a, b in pairs])
    y0 = [remote(window(g, 4), window(g, 2), up) for g in range(HALF)]
    y1 = [remote(window(g, 2), window(g, 0), up) for g in range(HALF)]
    z0 = [remote(window(g, 4 - 2 * zl), window(g, 3), zdev) for g in range(HALF)]
    z1 = [remote(window(g, 2 - 2 * zl), window(g, 1), zdev) for g in range(HALF)]
    in_rows = pl.ds(pl.multiple_of(x * T + k * 128, 128), 128)
    ins, shared = [], []
    for dx in (1, 2, 3):
        ins.append(remote(in_ref.at[:, rows_of(lax.rem(x + dx, 4), 1024)], inx.at[in_rows, :], xs[dx - 1]))
    for dx in (1, 2, 3):
        piece = inx.at[pl.ds(pl.multiple_of(lax.rem(x + 4 - dx, 4) * T + k * 128, 128), 128), :]
        shared.append(remote(piece, piece, sib))
    shared.append(remote(in_ref.at[:, rows_of(x, 1024)], inx.at[in_rows, :], sib))
    in_near = local(in_ref.at[:, rows_of(x, 1024)], inx.at[in_rows, :])
    w0 = remote(w_ref.at[pl.ds(pl.multiple_of(k * 1024 + x * T, T), T), :], wx.at[rows_of(x), :], (p, 1 - f))
    ws = [remote(wx.at[rows_of(x), :], wx.at[rows_of(x), :], device) for device in xs]
    w_near = local(w_ref.at[rows_of(k, 1024), :], wk)
    steps = 8 // HB * HALF
    width = HB * D
    gqs = [
        remote(dq.at[other, pl.ds(n * width, width)], gq_ref.at[:, pl.ds(pl.multiple_of(k * 4096 + n * width, width), width)], sib)
        for n in range(steps)
    ]
    gq_near = [
        local(dq.at[own, pl.ds(n * width, width)], gq_ref.at[:, pl.ds(pl.multiple_of(k * 4096 + n * width, width), width)])
        for n in range(steps)
    ]
    zc = [remote(zsend.at[g], zrecv.at[g], zdev) for g in range(HALF)]
    yc = [[remote(ysend.at[g, i], yrecv.at[g, i], down) for i in range(2)] for g in range(HALF)]
    across = [remote(cat.at[:, :, column(k, g, D)], cat.at[:, :, column(k, g, D)], sib) for g in range(HALF)]
    gxs = [[remote(gx.at[g, :, rows_of(x)], gx.at[g, :, rows_of(x)], device) for device in xs] for g in range(HALF)]
    gws = [[remote(gw_send.at[g, i], gw_recv.at[g, i], device) for i, device in enumerate(ys)] for g in range(HALF)]
    rzs = [[remote(last.at[g, i], rz.at[g, i], device) for i, device in enumerate(zs)] for g in range(HALF)]
    fins = [remote(fin.at[g, 1 - k], last_recv.at[g], sib) for g in range(HALF)]
    gi_cols = [rows_of((f if j == 0 else 1 - f) * 2 + k, 1024) for j in range(2)]
    gis = [remote(gibuf.at[j, other, :], gi_ref.at[:, gi_cols[j]], sib) for j in range(2)]
    gi_near = [local(gibuf.at[j, own, :], gi_ref.at[:, gi_cols[j]]) for j in range(2)]

    def start(copies):
        for c in copies:
            c.start()

    def arrived(copies):
        for c in copies:
            c.wait_recv()

    def ended(copies):
        for c in copies:
            c.wait()

    greet([sib, up, down] + xs + ys + zs)
    for g in range(HALF):
        start(kv[g] + kv_near[g])
        if g == 0:
            start(qs[0] + q_near[0])
    for g in range(1, HALF):
        start(qs[g] + q_near[g])
    start([w0, w_near, in_near, shared[3]] + ins)

    key_at = lax.broadcasted_iota(jnp.int32, (W, T), 0)
    query_at = lax.broadcasted_iota(jnp.int32, (W, T), 1)
    allowed = (key_doc[...] == query_doc[...]) & (key_at <= query_at + (W - T))
    bias[...] = jnp.where(allowed, 0.0, -1e30).astype(f32)

    def own_keys(g):
        arrived(kv[g])
        ended(kv_near[g])
        start([y0[g]])

    def pass_on(g):
        arrived([y0[g]])
        start([y1[g], z0[g]])

    def pass_last(g):
        arrived([y1[g]])
        start([z1[g]])

    def ready(g):
        arrived([z0[g], z1[g]] + qs[g])
        ended(q_near[g])

    own_keys(0)
    own_keys(1)
    pass_on(0)
    pass_on(1)
    pass_last(0)
    own_keys(2)
    own_keys(3)
    ready(0)

    def share_inputs():
        arrived(ins)
        start(shared[:3])

    def inputs_ready():
        arrived(shared)
        ended([in_near])

    def share_weight():
        arrived([w0])
        start(ws)

    before = {
        1: [lambda: pass_last(1), lambda: pass_on(2), lambda: pass_on(3)],
        2: [lambda: ready(1), lambda: pass_last(2), lambda: pass_last(3), share_weight],
        3: [share_inputs],
        4: [lambda: ready(2), inputs_ready],
        6: [lambda: ready(3)],
    }

    def block(index):
        return slice(index * T, (index + 1) * T)

    upper = zl == 1

    def back_z(g):
        for a, index in enumerate((3, 1)):
            zsend[g, a] = acc[g, :, block(index), :].astype(bf16)
        start([zc[g]])

    def back_y(g):
        arrived([zc[g]])
        ysend[g, 0] = (acc[g, :, block(0), :] + jnp.where(upper, zrecv[g, 1].astype(f32), 0.0)).astype(bf16)
        start([yc[g][0]])

    def back_yy(g):
        r0, r1 = zrecv[g, 0].astype(f32), zrecv[g, 1].astype(f32)
        arrived([yc[g][0]])
        part = acc[g, :, block(2), :] + jnp.where(upper, r0, r1) + yrecv[g, 0].astype(f32)
        ysend[g, 1] = part.astype(bf16)
        start([yc[g][1]])

    def owned(g):
        arrived([yc[g][1]])
        part = acc[g, :, block(4), :] + jnp.where(upper, 0.0, zrecv[g, 0].astype(f32)) + yrecv[g, 1].astype(f32)
        cat[0, :, column(k, g, D)] = (part[0] * SCALE).astype(bf16)
        cat[1, :, column(k, g, D)] = part[1].astype(bf16)
        gx[g, :, rows_of(x)] = part[1].T.astype(bf16)
        start(gxs[g] + [across[g]])

    def weight_part(g):
        arrived(gxs[g])
        for dy in (1, 2, 3, 0):
            part = jnp.dot(gx[g], inx[:, rows_of(lax.rem(y + dy, 4))], preferred_element_type=f32)
            if dy:
                gw_send[g, dy - 1] = part.astype(bf16)
                start([gws[g][dy - 1]])
            else:
                gw_own[g] = part

    def weight_y(g):
        arrived(gws[g])
        part = gw_own[g]
        for i in range(3):
            part += gw_recv[g, i].astype(f32)
        part = part.T.reshape(2, 2, 2, 32, D)
        for a in range(2):
            for c in range(2):
                zst[g, a, c] = part[a, :, c]
        for i in range(3):
            to_z, to_f = (zl, 1 - zl, 1 - zl)[i], (1 - f, f, 1 - f)[i]
            last[g, i] = zst[g, to_z, to_f].astype(bf16)
        start(rzs[g])

    def weight_z(g):
        arrived(rzs[g])
        part = zst[g, zl, f]
        for i in range(3):
            part += rz[g, i].astype(f32)
        fin[g] = part * (1.0 / math.sqrt(2 * 8192))
        start([fins[g]])

    stages = [back_z, back_y, back_yy, owned, weight_part, weight_y, weight_z]

    def after(n):
        per = steps // HALF
        return [(s, g) for s in range(len(stages)) for g in range(HALF) if n == per * (g + 1) - 1 + s]

    def body(step, carry):
        for n, acts in before.items():

            @pl.when(step == n)
            def _():
                for act in acts:
                    act()

        per = steps // HALF
        g, j = step // per, step % per

        @pl.when(j == 0)
        def _():
            kt[...] = slab[g, 0].T
            acc[g] = jnp.zeros((2, W, D), f32)

        for a in range(HB):
            cols = pl.ds(pl.multiple_of(step * width + a * D, D), D)
            q, do = qx[:, cols], dox[:, cols]
            s_ref, dp_ref, p_ref, ds_ref = scratch[4 * a : 4 * a + 4]
            grad, inverse = attend(q, do, slab.at[g, 0], slab.at[g, 1], kt, bias, s_ref, dp_ref, p_ref, ds_ref)
            dq[:, cols] = grad.astype(bf16)
            acc[g, 0] += jnp.dot(ds_ref[...], (q * inverse).astype(bf16), preferred_element_type=f32)
            acc[g, 1] += jnp.dot(p_ref[...], (do * inverse).astype(bf16), preferred_element_type=f32)

        for n in range(steps):

            @pl.when(step == n)
            def _():
                start([gqs[n], gq_near[n]])
                for s, g in after(n):
                    stages[s](g)

        return carry

    lax.fori_loop(0, steps, body, 0)

    def outputs():
        arrived(across + ws)
        ended([w_near])
        gk_ref[...] = cat[0, own, :]
        gv_ref[...] = cat[1, own, :]
        for j, w in enumerate((wk, wx)):
            for i in range(0, 1024, 256):
                gibuf[j, :, i : i + 256] = lax.dot_general(
                    cat[1], w[i : i + 256, :], NT, preferred_element_type=f32
                ).astype(bf16)
            start([gis[j], gi_near[j]])

    for n in range(steps, steps + len(stages) - 1):
        for s, g in after(n):
            if stages[s] is weight_part and g == HALF - 1:
                outputs()
            stages[s](g)
    for g in range(HALF):
        gw_ref[:, column(k, g, D)] = fin[g, k]
    arrived(fins)
    for g in range(HALF):
        gw_ref[:, column(1 - k, g, D)] = last_recv[g]
    arrived(gqs + gis)
    ended(gq_near + gi_near)
    for c in every:
        c.wait_send()


def backward(key_doc, query_doc, queries, out_grad, keys, values, inputs, weight):
    pair = (2, T, D)
    scratch = [
        pltpu.VMEM((T, 4096), bf16),
        pltpu.VMEM((T, 4096), bf16),
        pltpu.VMEM((HALF, 2, W, D), bf16),
        pltpu.VMEM((1024, 1024), bf16),
        pltpu.VMEM((1024, 1024), bf16),
        pltpu.VMEM((1024, 1024), bf16),
        pltpu.VMEM((T, 4096), bf16),
        pltpu.VMEM((HALF, 2, W, D), f32),
        pltpu.VMEM((D, W), bf16),
        pltpu.VMEM((W, T), f32),
        pltpu.VMEM((HALF, 2) + pair, bf16),
        pltpu.VMEM((HALF, 2) + pair, bf16),
        pltpu.VMEM((HALF, 2) + pair, bf16),
        pltpu.VMEM((HALF, 2) + pair, bf16),
        pltpu.VMEM((2, T, 1024), bf16),
        pltpu.VMEM((HALF, D, 1024), bf16),
        pltpu.VMEM((2, T, 1024), bf16),
        pltpu.VMEM((HALF, 3, D, T), bf16),
        pltpu.VMEM((HALF, 3, D, T), bf16),
        pltpu.VMEM((HALF, D, T), f32),
        pltpu.VMEM((HALF, 2, 2, 2, 32, D), f32),
        pltpu.VMEM((HALF, 3, 2, 32, D), bf16),
        pltpu.VMEM((HALF, 3, 2, 32, D), bf16),
        pltpu.VMEM((HALF, 2, 32, D), f32),
        pltpu.VMEM((HALF, 32, D), f32),
        pltpu.SemaphoreType.DMA((MESSAGES,)),
        pltpu.SemaphoreType.DMA((MESSAGES,)),
        pltpu.SemaphoreType.DMA((28,)),
    ]
    for _ in range(HB):
        scratch += [pltpu.VMEM((W, T), t) for t in (f32, f32, bf16, bf16)]
    return pl.pallas_call(
        kernel,
        out_shape=[
            jax.ShapeDtypeStruct((128, 8192), bf16),
            jax.ShapeDtypeStruct((128, 1024), bf16),
            jax.ShapeDtypeStruct((128, 1024), bf16),
            jax.ShapeDtypeStruct((128, 4096), bf16),
            jax.ShapeDtypeStruct((32, 1024), f32),
        ],
        in_specs=[VMEM, VMEM] + [ANY] * 6,
        out_specs=[ANY, VMEM, VMEM, ANY, VMEM],
        scratch_shapes=scratch,
        compiler_params=pltpu.CompilerParams(collective_id=0, has_side_effects=True, vmem_limit_bytes=60 * 2**20),
        name="backward",
    )(key_doc, query_doc, queries, out_grad, keys, values, inputs, weight)


def documents(lengths):
    chip = lax.axis_index("seq") // 2
    entry = jnp.arange(lengths.shape[0])
    bounds = jnp.sum(jnp.where(entry[None, :] <= entry[:, None], lengths[None, :], 0), axis=1)
    at = chip * T - (W - T) + jnp.arange(W, dtype=jnp.int32)
    ids = jnp.sum((at[:, None] >= bounds[None, :]).astype(jnp.int32), axis=1)
    return jnp.where(at < 0, -1, ids)


def local(queries, keys, values, out_grad, doc_lengths, inputs, value_weight):
    ids = documents(doc_lengths[0])
    gq, gk, gv, gi, gw = backward(
        ids[:, None], ids[None, W - T :], queries[0], out_grad[0], keys[0], values[0], inputs[0], value_weight
    )
    return gq[None], gk[None], gv[None], gi[None], gw


def solution(mesh):
    tokens = P("fsdp", "seq", None)
    in_specs = (tokens, tokens, tokens, tokens, P("fsdp", None), tokens, P("fsdp", None))
    out_specs = (tokens, tokens, tokens, tokens, P(("seq", "fsdp"), None))
    return jax.shard_map(local, mesh=mesh, in_specs=in_specs, out_specs=out_specs, check_vma=False)
```

time: 1200 us -> 146 us (0.12)
  waiting for transfers between devices: 867 us -> 0 us
  matrix products: 140 us -> 0 us
  Pallas kernels: 0 us -> 137 us
  local copies, waits for them, and re-layouts: 95.7 us -> 6.26 us
  starting transfers between devices: 51.3 us -> 0 us
  other arithmetic: 24.8 us -> 2.52 us
  between operations: 15.8 us -> 0.7 us
    unnamed x4 -> x0, waiting for transfers between devices: 652 us -> none
    ppermute x16 -> x0, waiting for transfers between devices: 190 us -> none  [shifted(): return lax.ppermute(value, axis, pairs)]
    pallas_call x0 -> x1, Pallas kernels: none -> 137 us  [backward(): pl.pallas_call(kernel, out_shape=[jax.ShapeDtypeStruct((128, 8192), bf16)...]
    dot_general x35 -> x0, matrix products: 95 us -> none  [the longest x8 27.7 us: group_backward(): jnp.einsum('qhd,kd->hqk', grad_group, value_slab, preferred_element_type=...]
    ppermute x16 -> x0, starting transfers between devices: 51.2 us -> none  [shifted(): return lax.ppermute(value, axis, pairs)]
    sub x8 -> x0, matrix products: 45.5 us -> none  [group_backward(): weights = jnp.where(allowed[None], jnp.exp(scores - row_max), 0.0)]
    unnamed x33 -> x13, local copies, waits for them, and re-layouts: 45.4 us -> 6.26 us
    all_gather x2 -> x0, waiting for transfers between devices: 24.5 us -> none  [piecewise(): done.append(jax.vmap(apply)(lax.all_gather(piece, axis), starts))]
  transfers between devices with their start and end apart: 19 -> 0, of which waited for: 17 -> 0; matrix products, arithmetic and copies ran while one was open for 5% -> 0% of each run, Pallas kernels for 0% -> 0%
where the time goes in v2:
time: 146 us
  Pallas kernels  137 us (94%)
  local copies, waits for them, and re-layouts  6.26 us (4%)
  other arithmetic  2.52 us (2%)
    pallas_call x1, Pallas kernels, backward(): pl.pallas_call(kernel, out_shape=[jax.ShapeDtypeStruct((128, 8192), bf16)...  137 us
    unnamed x13, local copies, waits for them, and re-layouts  6.26 us

profile of v2, /device:TPU:1, one launch (start us, length us, event | category | flops | bytes accessed | tf_op | source)
XLA Modules:
  0.0 146.1 jit_solution(5381212429222800414)
XLA Ops:
  0.6 0.8 select_reduce_fusion
  1.4 0.1 convert_reduce_fusion
  1.5 0.6 compare_select_fusion
  2.1 1.1 reshape_select_fusion.key_doc
  3.2 136.6 %backward.1 = (bf16[128,8192]{1,0:T(8,128)(2,1)}, bf16[128,1024]{1,0:T(8,128)(2,1)}, bf16[128,1024]{1,0:T(8,128)(2,1)}, bf16[128,4096]{1,0:T(8,128)(2,1)}, f32[32,1024]{1,0:T(8,128)}) custom-call(s32[1280,1]{1,0:T(8,128)} %reshape_select_fusion.key_doc, s32[1,256]{1,0:T(1,128)} %bitcast.20, bf16[128,8192]{1,0:T(8,128)(2,1)} %bitcast.12, ...), custom_call_target="tpu_custom_call" | custom-call | tf_op jit(solution)/shard_map/backward/pallas_call | solution.py:401
  139.8 0.0 copy-start.2
  139.8 0.0 copy-start.1
  139.8 0.0 copy-start
  139.8 3.2 %copy.19 = bf16[1,128,8192]{2,1,0:T(8,128)(2,1)} copy(bf16[1,128,8192]{2,1,0:T(8,128)(2,1)} %bitcast.11) | data formatting | bytes 4194304
  143.0 0.0 copy-done.2
  143.0 0.0 copy-start.3
  143.0 0.7 copy.20
  143.7 0.0 copy-done.1
  143.7 0.7 copy.21
  144.4 0.0 copy-done
  144.5 1.0 copy.22
  145.4 0.0 copy-done.3
  145.4 0.7 copy.23
  (1 shorter events, 0.0 us)
Async XLA Ops:
  139.8 3.2 %copy-start.2 = (bf16[128,1024]{1,0:T(8,128)(2,1)S(1)}, bf16[128,1024]{1,0:T(8,128)(2,1)}, u32[]{:S(2)}) copy-start(bf16[128,1024]{1,0:T(8,128)(2,1)} %get-tuple-element.11) | copy-start | bytes 786436
  139.8 3.9 %copy-start.1 = (bf16[128,1024]{1,0:T(8,128)(2,1)S(1)}, bf16[128,1024]{1,0:T(8,128)(2,1)}, u32[]{:S(2)}) copy-start(bf16[128,1024]{1,0:T(8,128)(2,1)} %get-tuple-element.12) | copy-start | bytes 786436
  139.8 4.6 %copy-start = (bf16[128,4096]{1,0:T(8,128)(2,1)S(1)}, bf16[128,4096]{1,0:T(8,128)(2,1)}, u32[]{:S(2)}) copy-start(bf16[128,4096]{1,0:T(8,128)(2,1)} %get-tuple-element.13) | copy-start | bytes 3145732
  143.0 2.4 %copy-start.3 = (f32[32,1024]{1,0:T(8,128)S(1)}, f32[32,1024]{1,0:T(8,128)}, u32[]{:S(2)}) copy-start(f32[32,1024]{1,0:T(8,128)} %get-tuple-element.24) | copy-start | bytes 393220

commit v3 on v2

--- a/solution.py
+++ b/solution.py
@@ -12,7 +12,7 @@
 W = 1280
 HALF = 4
 HB = 4
-MESSAGES = 109
+MESSAGES = 114
 SCALE = 1.0 / math.sqrt(D)
 EXP2 = math.log2(math.e) * SCALE
 NT = (((1,), (1,)), ((), ()))
@@ -78,7 +78,7 @@
 def kernel(
     key_doc, query_doc, q_in, do_in, k_in, v_in, in_ref, w_ref,
     gq_ref, gk_ref, gv_ref, gi_ref, gw_ref,
-    qx, dox, slab, inx, wk, wx, dq, acc, kt, bias,
+    qx, dox, slab, inx, wk, dq, acc, kt, bias,
     zsend, zrecv, ysend, yrecv, cat, gx, gibuf, gw_send, gw_recv, gw_own, zst, last, rz, fin, last_recv,
     send, recv, near, *scratch,
 ):
@@ -135,8 +135,6 @@
         shared.append(remote(piece, piece, sib))
     shared.append(remote(in_ref.at[:, rows_of(x, 1024)], inx.at[in_rows, :], sib))
     in_near = local(in_ref.at[:, rows_of(x, 1024)], inx.at[in_rows, :])
-    w0 = remote(w_ref.at[pl.ds(pl.multiple_of(k * 1024 + x * T, T), T), :], wx.at[rows_of(x), :], (p, 1 - f))
-    ws = [remote(wx.at[rows_of(x), :], wx.at[rows_of(x), :], device) for device in xs]
     w_near = local(w_ref.at[rows_of(k, 1024), :], wk)
     steps = 8 // HB * HALF
     width = HB * D
@@ -150,14 +148,21 @@
     ]
     zc = [remote(zsend.at[g], zrecv.at[g], zdev) for g in range(HALF)]
     yc = [[remote(ysend.at[g, i], yrecv.at[g, i], down) for i in range(2)] for g in range(HALF)]
-    across = [remote(cat.at[:, :, column(k, g, D)], cat.at[:, :, column(k, g, D)], sib) for g in range(HALF)]
+    first2 = pl.ds(0, 2)
+    across = [remote(cat.at[first2, :, column(k, g, D)], cat.at[first2, :, column(k, g, D)], sib) for g in range(HALF)]
+    cross = [remote(cat.at[1, :, column(k, g, D)], cat.at[2, :, column(k, g, D)], (p, 1 - f)) for g in range(HALF)]
+    relay = [remote(cat.at[2, :, column(k, g, D)], cat.at[2, :, column(k, g, D)], sib) for g in range(HALF)]
     gxs = [[remote(gx.at[g, :, rows_of(x)], gx.at[g, :, rows_of(x)], device) for device in xs] for g in range(HALF)]
     gws = [[remote(gw_send.at[g, i], gw_recv.at[g, i], device) for i, device in enumerate(ys)] for g in range(HALF)]
     rzs = [[remote(last.at[g, i], rz.at[g, i], device) for i, device in enumerate(zs)] for g in range(HALF)]
     fins = [remote(fin.at[g, 1 - k], last_recv.at[g], sib) for g in range(HALF)]
-    gi_cols = [rows_of((f if j == 0 else 1 - f) * 2 + k, 1024) for j in range(2)]
-    gis = [remote(gibuf.at[j, other, :], gi_ref.at[:, gi_cols[j]], sib) for j in range(2)]
-    gi_near = [local(gibuf.at[j, own, :], gi_ref.at[:, gi_cols[j]]) for j in range(2)]
+    gi_cols = rows_of(f * 2 + k, 1024)
+    gis = [
+        remote(gibuf.at[1, own, :], gi_ref.at[:, gi_cols], (p, 1 - f)),
+        remote(gibuf.at[1, other, :], gi_ref.at[:, gi_cols], (p + 1 - 2 * k, 1 - f)),
+        remote(gibuf.at[0, other, :], gi_ref.at[:, gi_cols], sib),
+    ]
+    gi_near = local(gibuf.at[0, own, :], gi_ref.at[:, gi_cols])
 
     def start(copies):
         for c in copies:
@@ -171,14 +176,14 @@
         for c in copies:
             c.wait()
 
-    greet([sib, up, down] + xs + ys + zs)
+    greet([sib, up, down, (p + 1 - 2 * k, 1 - f)] + xs + ys + zs)
     for g in range(HALF):
         start(kv[g] + kv_near[g])
         if g == 0:
             start(qs[0] + q_near[0])
     for g in range(1, HALF):
         start(qs[g] + q_near[g])
-    start([w0, w_near, in_near, shared[3]] + ins)
+    start([w_near, in_near])
 
     key_at = lax.broadcasted_iota(jnp.int32, (W, T), 0)
     query_at = lax.broadcasted_iota(jnp.int32, (W, T), 1)
@@ -219,13 +224,12 @@
         arrived(shared)
         ended([in_near])
 
-    def share_weight():
-        arrived([w0])
-        start(ws)
+    def send_inputs():
+        start(ins + shared[3:])
 
     before = {
-        1: [lambda: pass_last(1), lambda: pass_on(2), lambda: pass_on(3)],
-        2: [lambda: ready(1), lambda: pass_last(2), lambda: pass_last(3), share_weight],
+        1: [send_inputs, lambda: pass_last(1), lambda: pass_on(2), lambda: pass_on(3)],
+        2: [lambda: ready(1), lambda: pass_last(2), lambda: pass_last(3)],
         3: [share_inputs],
         4: [lambda: ready(2), inputs_ready],
         6: [lambda: ready(3)],
@@ -259,9 +263,12 @@
         cat[0, :, column(k, g, D)] = (part[0] * SCALE).astype(bf16)
         cat[1, :, column(k, g, D)] = part[1].astype(bf16)
         gx[g, :, rows_of(x)] = part[1].T.astype(bf16)
-        start(gxs[g] + [across[g]])
+        start([across[g], cross[g]] + gxs[g])
 
     def weight_part(g):
+        if g < HALF - 1:
+            arrived([cross[g]])
+            start([relay[g]])
         arrived(gxs[g])
         for dy in (1, 2, 3, 0):
             part = jnp.dot(gx[g], inx[:, rows_of(lax.rem(y + dy, 4))], preferred_element_type=f32)
@@ -337,16 +344,18 @@
     lax.fori_loop(0, steps, body, 0)
 
     def outputs():
-        arrived(across + ws)
+        arrived([cross[HALF - 1]])
+        start([relay[HALF - 1]])
         ended([w_near])
+        arrived(across + relay)
+        for j in (1, 0):
+            for i in range(0, 1024, 256):
+                gibuf[j, :, i : i + 256] = lax.dot_general(
+                    cat[1 + j], wk[i : i + 256, :], NT, preferred_element_type=f32
+                ).astype(bf16)
+            start(gis[:2] if j else [gis[2], gi_near])
         gk_ref[...] = cat[0, own, :]
         gv_ref[...] = cat[1, own, :]
-        for j, w in enumerate((wk, wx)):
-            for i in range(0, 1024, 256):
-                gibuf[j, :, i : i + 256] = lax.dot_general(
-                    cat[1], w[i : i + 256, :], NT, preferred_element_type=f32
-                ).astype(bf16)
-            start([gis[j], gi_near[j]])
 
     for n in range(steps, steps + len(stages) - 1):
         for s, g in after(n):
@@ -359,7 +368,7 @@
     for g in range(HALF):
         gw_ref[:, column(1 - k, g, D)] = last_recv[g]
     arrived(gqs + gis)
-    ended(gq_near + gi_near)
+    ended(gq_near + [gi_near])
     for c in every:
         c.wait_send()
 
@@ -370,7 +379,6 @@
         pltpu.VMEM((T, 4096), bf16),
         pltpu.VMEM((T, 4096), bf16),
         pltpu.VMEM((HALF, 2, W, D), bf16),
-        pltpu.VMEM((1024, 1024), bf16),
         pltpu.VMEM((1024, 1024), bf16),
         pltpu.VMEM((1024, 1024), bf16),
         pltpu.VMEM((T, 4096), bf16),
@@ -381,7 +389,7 @@
         pltpu.VMEM((HALF, 2) + pair, bf16),
         pltpu.VMEM((HALF, 2) + pair, bf16),
         pltpu.VMEM((HALF, 2) + pair, bf16),
-        pltpu.VMEM((2, T, 1024), bf16),
+        pltpu.VMEM((3, T, 1024), bf16),
         pltpu.VMEM((HALF, D, 1024), bf16),
         pltpu.VMEM((2, T, 1024), bf16),
         pltpu.VMEM((HALF, 3, D, T), bf16),
@@ -394,7 +402,7 @@
         pltpu.VMEM((HALF, 32, D), f32),
         pltpu.SemaphoreType.DMA((MESSAGES,)),
         pltpu.SemaphoreType.DMA((MESSAGES,)),
-        pltpu.SemaphoreType.DMA((28,)),
+        pltpu.SemaphoreType.DMA((27,)),
     ]
     for _ in range(HB):
         scratch += [pltpu.VMEM((W, T), t) for t in (f32, f32, bf16, bf16)]
@@ -415,6 +423,32 @@
     )(key_doc, query_doc, queries, out_grad, keys, values, inputs, weight)
 
 
+def place_kernel(*refs):
+    n = (len(refs) - 2) // 3
+    inward = [pltpu.make_async_copy(refs[i], refs[2 * n + i], refs[-2].at[i]) for i in range(n)]
+    outward = [pltpu.make_async_copy(refs[2 * n + i], refs[n + i], refs[-1].at[i]) for i in range(n)]
+    for c in inward:
+        c.start()
+    for i, c in enumerate(inward):
+        c.wait()
+        outward[i].start()
+    for c in outward:
+        c.wait()
+
+
+def place(arrays):
+    n = len(arrays)
+    return pl.pallas_call(
+        place_kernel,
+        out_shape=[jax.ShapeDtypeStruct(a.shape, a.dtype) for a in arrays],
+        in_specs=[ANY] * n,
+        out_specs=[ANY] * n,
+        scratch_shapes=[pltpu.VMEM(a.shape, a.dtype) for a in arrays] + [pltpu.SemaphoreType.DMA((n,))] * 2,
+        compiler_params=pltpu.CompilerParams(vmem_limit_bytes=16 * 2**20),
+        name="place",
+    )(*arrays)
+
+
 def documents(lengths):
     chip = lax.axis_index("seq") // 2
     entry = jnp.arange(lengths.shape[0])
@@ -426,9 +460,10 @@
 
 def local(queries, keys, values, out_grad, doc_lengths, inputs, value_weight):
     ids = documents(doc_lengths[0])
-    gq, gk, gv, gi, gw = backward(
+    arrays = backward(
         ids[:, None], ids[None, W - T :], queries[0], out_grad[0], keys[0], values[0], inputs[0], value_weight
     )
+    gq, gk, gv, gi, gw = place(arrays)
     return gq[None], gk[None], gv[None], gi[None], gw
 
 

time: 146 us -> 140 us (0.959)
  Pallas kernels: 137 us -> 131 us
    pallas_call x1, Pallas kernels: 137 us -> 128 us  [backward(): pl.pallas_call(kernel, out_shape=[jax.ShapeDtypeStruct((128, 8192), bf16)...]
    pallas_call x0 -> x1, Pallas kernels: none -> 2.36 us  [place(): pl.pallas_call(place_kernel, out_shape=[jax.ShapeDtypeStruct(a.shape, a.d...]
    unnamed x13 -> x10, local copies, waits for them, and re-layouts: 6.26 us -> 5.61 us
where the time goes in v3:
time: 140 us
  Pallas kernels  131 us (94%)
  local copies, waits for them, and re-layouts  5.61 us (4%)
  other arithmetic  2.52 us (2%)
    pallas_call x1, Pallas kernels, backward(): pl.pallas_call(kernel, out_shape=[jax.ShapeDtypeStruct((128, 8192), bf16)...  128 us
    unnamed x10, local copies, waits for them, and re-layouts  5.61 us

profile of v3, /device:TPU:1, one launch (start us, length us, event | category | flops | bytes accessed | tf_op | source)
XLA Modules:
  0.0 139.6 jit_solution(11898994024260403727)
XLA Ops:
  0.6 0.8 select_reduce_fusion
  1.4 0.1 convert_reduce_fusion
  1.5 0.6 compare_select_fusion
  2.1 1.1 reshape_select_fusion.key_doc
  3.2 128.4 %backward.1 = (bf16[128,8192]{1,0:T(8,128)(2,1)}, bf16[128,1024]{1,0:T(8,128)(2,1)}, bf16[128,1024]{1,0:T(8,128)(2,1)}, bf16[128,4096]{1,0:T(8,128)(2,1)}, f32[32,1024]{1,0:T(8,128)}) custom-call(s32[1280,1]{1,0:T(8,128)} %reshape_select_fusion.key_doc, s32[1,256]{1,0:T(1,128)} %bitcast.16, bf16[128,8192]{1,0:T(8,128)(2,1)} %bitcast.11, ...), custom_call_target="tpu_custom_call" | custom-call | tf_op jit(solution)/shard_map/backward/pallas_call | solution.py:409
  131.6 0.0 copy-start
  131.6 1.6 %copy-done = bf16[128,8192]{1,0:T(8,128)(2,1)S(1)} copy-done((bf16[128,8192]{1,0:T(8,128)(2,1)S(1)}, bf16[128,8192]{1,0:T(8,128)(2,1)}, u32[]{:S(2)}) %copy-start) | copy-done | bytes 2097176
  133.2 0.0 copy-start.1
  133.2 1.2 copy-done.1
  134.4 0.0 copy-start.2
  134.4 0.9 copy-done.2
  135.4 0.0 copy-start.3
  135.4 0.9 copy-done.3
  136.3 0.0 copy-start.4
  136.3 0.9 copy-done.4
  137.2 2.4 %place.1 = (bf16[128,8192]{1,0:T(8,128)(2,1)}, bf16[128,1024]{1,0:T(8,128)(2,1)}, bf16[128,1024]{1,0:T(8,128)(2,1)}, bf16[128,4096]{1,0:T(8,128)(2,1)}, f32[32,1024]{1,0:T(8,128)}) custom-call(bf16[128,8192]{1,0:T(8,128)(2,1)S(1)} %copy-done, bf16[128,1024]{1,0:T(8,128)(2,1)S(1)} %copy-done.2, bf16[128,1024]{1,0:T(8,128)(2,1)S(1)} %copy-done.3, ...), custom_call_target="tpu_custom_call" | custom-call | tf_op jit(solution)/shard_map/place/pallas_call | solution.py:441
  (1 shorter events, 0.0 us)
Async XLA Ops:
  131.6 1.6 %copy-start = (bf16[128,8192]{1,0:T(8,128)(2,1)S(1)}, bf16[128,8192]{1,0:T(8,128)(2,1)}, u32[]{:S(2)}) copy-start(bf16[128,8192]{1,0:T(8,128)(2,1)} %get-tuple-element.15.refs_0_) | copy-start | bytes 6291460
  133.2 1.2 copy-start.1
  134.4 0.9 copy-start.2
  135.4 0.9 copy-start.3
  136.3 0.9 copy-start.4

commit v4 on v3

--- a/solution.py
+++ b/solution.py
@@ -12,7 +12,7 @@
 W = 1280
 HALF = 4
 HB = 4
-MESSAGES = 114
+MESSAGES = 130
 SCALE = 1.0 / math.sqrt(D)
 EXP2 = math.log2(math.e) * SCALE
 NT = (((1,), (1,)), ((), ()))
@@ -146,10 +146,13 @@
         local(dq.at[own, pl.ds(n * width, width)], gq_ref.at[:, pl.ds(pl.multiple_of(k * 4096 + n * width, width), width)])
         for n in range(steps)
     ]
-    zc = [remote(zsend.at[g], zrecv.at[g], zdev) for g in range(HALF)]
-    yc = [[remote(ysend.at[g, i], yrecv.at[g, i], down) for i in range(2)] for g in range(HALF)]
-    first2 = pl.ds(0, 2)
-    across = [remote(cat.at[first2, :, column(k, g, D)], cat.at[first2, :, column(k, g, D)], sib) for g in range(HALF)]
+    zc = [[remote(zsend.at[g, c], zrecv.at[g, c], zdev) for c in range(2)] for g in range(HALF)]
+    yc = [
+        [[remote(ysend.at[g, i, c], yrecv.at[g, i, c], down) for c in range(2)] for i in range(2)] for g in range(HALF)
+    ]
+    across = [
+        [remote(cat.at[c, :, column(k, g, D)], cat.at[c, :, column(k, g, D)], sib) for c in range(2)] for g in range(HALF)
+    ]
     cross = [remote(cat.at[1, :, column(k, g, D)], cat.at[2, :, column(k, g, D)], (p, 1 - f)) for g in range(HALF)]
     relay = [remote(cat.at[2, :, column(k, g, D)], cat.at[2, :, column(k, g, D)], sib) for g in range(HALF)]
     gxs = [[remote(gx.at[g, :, rows_of(x)], gx.at[g, :, rows_of(x)], device) for device in xs] for g in range(HALF)]
@@ -241,29 +244,49 @@
     upper = zl == 1
 
     def back_z(g):
-        for a, index in enumerate((3, 1)):
-            zsend[g, a] = acc[g, :, block(index), :].astype(bf16)
-        start([zc[g]])
+        for c in (1, 0):
+            for a, index in enumerate((3, 1)):
+                zsend[g, c, a] = acc[g, c, block(index), :].astype(bf16)
+            start([zc[g][c]])
+
+    def hop_y(g, c):
+        arrived([zc[g][c]])
+        ysend[g, 0, c] = (acc[g, c, block(0), :] + jnp.where(upper, zrecv[g, c, 1].astype(f32), 0.0)).astype(bf16)
+        start([yc[g][0][c]])
+
+    def hop_yy(g, c):
+        arrived([yc[g][0][c]])
+        r0, r1 = zrecv[g, c, 0].astype(f32), zrecv[g, c, 1].astype(f32)
+        part = acc[g, c, block(2), :] + jnp.where(upper, r0, r1) + yrecv[g, 0, c].astype(f32)
+        ysend[g, 1, c] = part.astype(bf16)
+        start([yc[g][1][c]])
+
+    def keep(g, c):
+        arrived([yc[g][1][c]])
+        r0 = jnp.where(upper, 0.0, zrecv[g, c, 0].astype(f32))
+        part = acc[g, c, block(4), :] + r0 + yrecv[g, 1, c].astype(f32)
+        if c:
+            cat[1, :, column(k, g, D)] = part.astype(bf16)
+            gx[g, :, rows_of(x)] = part.T.astype(bf16)
+            start([across[g][1], cross[g]] + gxs[g])
+        else:
+            cat[0, :, column(k, g, D)] = (part * SCALE).astype(bf16)
+            start([across[g][0]])
+
+    def both(hop, g):
+        for c in (1, 0) if g < HALF - 1 else (1,):
+            hop(g, c)
 
     def back_y(g):
-        arrived([zc[g]])
-        ysend[g, 0] = (acc[g, :, block(0), :] + jnp.where(upper, zrecv[g, 1].astype(f32), 0.0)).astype(bf16)
-        start([yc[g][0]])
+        both(hop_y, g)
 
     def back_yy(g):
-        r0, r1 = zrecv[g, 0].astype(f32), zrecv[g, 1].astype(f32)
-        arrived([yc[g][0]])
-        part = acc[g, :, block(2), :] + jnp.where(upper, r0, r1) + yrecv[g, 0].astype(f32)
-        ysend[g, 1] = part.astype(bf16)
-        start([yc[g][1]])
+        both(hop_yy, g)
 
     def owned(g):
-        arrived([yc[g][1]])
-        part = acc[g, :, block(4), :] + jnp.where(upper, 0.0, zrecv[g, 0].astype(f32)) + yrecv[g, 1].astype(f32)
-        cat[0, :, column(k, g, D)] = (part[0] * SCALE).astype(bf16)
-        cat[1, :, column(k, g, D)] = part[1].astype(bf16)
-        gx[g, :, rows_of(x)] = part[1].T.astype(bf16)
-        start([across[g], cross[g]] + gxs[g])
+        both(keep, g)
+        if g == HALF - 1:
+            hop_y(g, 0)
 
     def weight_part(g):
         if g < HALF - 1:
@@ -347,21 +370,25 @@
         arrived([cross[HALF - 1]])
         start([relay[HALF - 1]])
         ended([w_near])
-        arrived(across + relay)
+        arrived(relay + [c[1] for c in across])
         for j in (1, 0):
             for i in range(0, 1024, 256):
                 gibuf[j, :, i : i + 256] = lax.dot_general(
                     cat[1 + j], wk[i : i + 256, :], NT, preferred_element_type=f32
                 ).astype(bf16)
             start(gis[:2] if j else [gis[2], gi_near])
-        gk_ref[...] = cat[0, own, :]
         gv_ref[...] = cat[1, own, :]
 
     for n in range(steps, steps + len(stages) - 1):
         for s, g in after(n):
             if stages[s] is weight_part and g == HALF - 1:
                 outputs()
+                hop_yy(g, 0)
             stages[s](g)
+            if stages[s] is weight_part and g == HALF - 1:
+                keep(g, 0)
+    arrived([c[0] for c in across])
+    gk_ref[...] = cat[0, own, :]
     for g in range(HALF):
         gw_ref[:, column(k, g, D)] = fin[g, k]
     arrived(fins)

time: 140 us -> 137 us (0.979)
  Pallas kernels: 131 us -> 128 us
    pallas_call x1, Pallas kernels: 128 us -> 125 us  [backward(): pl.pallas_call(kernel, out_shape=[jax.ShapeDtypeStruct((128, 8192), bf16)...]
where the time goes in v4:
time: 137 us
  Pallas kernels  128 us (93%)
  local copies, waits for them, and re-layouts  5.61 us (4%)
  other arithmetic  2.52 us (2%)
    pallas_call x1, Pallas kernels, backward(): pl.pallas_call(kernel, out_shape=[jax.ShapeDtypeStruct((128, 8192), bf16)...  125 us
    unnamed x10, local copies, waits for them, and re-layouts  5.61 us

profile of v4, /device:TPU:1, one launch (start us, length us, event | category | flops | bytes accessed | tf_op | source)
XLA Modules:
  0.0 136.8 jit_solution(16242998819954013466)
XLA Ops:
  0.6 0.8 select_reduce_fusion
  1.4 0.1 convert_reduce_fusion
  1.5 0.6 compare_select_fusion
  2.1 1.1 reshape_select_fusion.key_doc
  3.2 125.4 %backward.1 = (bf16[128,8192]{1,0:T(8,128)(2,1)}, bf16[128,1024]{1,0:T(8,128)(2,1)}, bf16[128,1024]{1,0:T(8,128)(2,1)}, bf16[128,4096]{1,0:T(8,128)(2,1)}, f32[32,1024]{1,0:T(8,128)}) custom-call(s32[1280,1]{1,0:T(8,128)} %reshape_select_fusion.key_doc, s32[1,256]{1,0:T(1,128)} %bitcast.16, bf16[128,8192]{1,0:T(8,128)(2,1)} %bitcast.11, ...), custom_call_target="tpu_custom_call" | custom-call | tf_op jit(solution)/shard_map/backward/pallas_call | solution.py:436
  128.6 0.0 copy-start
  128.6 1.6 %copy-done = bf16[128,8192]{1,0:T(8,128)(2,1)S(1)} copy-done((bf16[128,8192]{1,0:T(8,128)(2,1)S(1)}, bf16[128,8192]{1,0:T(8,128)(2,1)}, u32[]{:S(2)}) %copy-start) | copy-done | bytes 2097176
  130.2 0.0 copy-start.1
  130.2 1.2 copy-done.1
  131.5 0.0 copy-start.2
  131.5 0.9 copy-done.2
  132.4 0.0 copy-start.3
  132.4 0.9 copy-done.3
  133.4 0.0 copy-start.4
  133.4 0.9 copy-done.4
  134.3 2.4 %place.1 = (bf16[128,8192]{1,0:T(8,128)(2,1)}, bf16[128,1024]{1,0:T(8,128)(2,1)}, bf16[128,1024]{1,0:T(8,128)(2,1)}, bf16[128,4096]{1,0:T(8,128)(2,1)}, f32[32,1024]{1,0:T(8,128)}) custom-call(bf16[128,8192]{1,0:T(8,128)(2,1)S(1)} %copy-done, bf16[128,1024]{1,0:T(8,128)(2,1)S(1)} %copy-done.2, bf16[128,1024]{1,0:T(8,128)(2,1)S(1)} %copy-done.3, ...), custom_call_target="tpu_custom_call" | custom-call | tf_op jit(solution)/shard_map/place/pallas_call | solution.py:468
  (1 shorter events, 0.0 us)
Async XLA Ops:
  128.6 1.6 %copy-start = (bf16[128,8192]{1,0:T(8,128)(2,1)S(1)}, bf16[128,8192]{1,0:T(8,128)(2,1)}, u32[]{:S(2)}) copy-start(bf16[128,8192]{1,0:T(8,128)(2,1)} %get-tuple-element.15.refs_0_) | copy-start | bytes 6291460
  130.2 1.2 copy-start.1
  131.5 0.9 copy-start.2
  132.4 0.9 copy-start.3
  133.4 0.9 copy-start.4
